TPU v7x, 32 devices: a whole 2x2x4 slice. The times are simulated.
32 devices in a mesh: seq: 4 (over y, x), tensor: 8 (over z, core).
Axes of the slice: x: 2, y: 2, z: 4, core: 2. Of those that a mesh axis runs over, the one named last changes fastest.
Arguments:
- tokens: bfloat16 [1024, 4096], P(('seq', 'tensor')), may hold values from -6 to 6
- w_gate: bfloat16 [4096, 8192], P('seq', 'tensor'), may hold values from -0.09375 to 0.09375
- w_xin: bfloat16 [4096, 8192], P('seq', 'tensor'), may hold values from -0.09375 to 0.09375
- w_bc: bfloat16 [4096, 2048], P('seq', 'tensor'), may hold values from -0.09375 to 0.09375
- w_dt: bfloat16 [4096, 128], P('seq', 'tensor'), may hold values from -0.09375 to 0.09375
- conv_x: float32 [4, 8192], P(None, 'tensor'), may hold values from -3 to 3
- conv_x_bias: float32 [8192], P('tensor'), may hold values from -3 to 3
- conv_bc: float32 [4, 2048], P(None, 'tensor'), may hold values from -3 to 3
- conv_bc_bias: float32 [2048], P('tensor'), may hold values from -3 to 3
- dt_bias: float32 [128], P('tensor'), may hold values from -1 to 1
- decay_rate: float32 [128], P('tensor'), may hold values from 0.000390625 to 0.08, as said below
- d_skip: float32 [128], P('tensor'), may hold values from 0.5 to 1.5
- norm_gain: float32 [8192], P('tensor'), may hold values from 0.25 to 1.75
- w_out: bfloat16 [8192, 4096], P('tensor', 'seq'), may hold values from -0.0625 to 0.0625
- lengths: int32 [8], replicated, may hold values from 1 to 512, 1024 in all
Outputs:
- mixed: bfloat16 [1024, 4096], P(('seq', 'tensor'))
Inputs may be any that keep to these rules, and one draw needn't show every extreme that they name: lengths of 8 prompts that fill the pack of 1024 tokens exactly; the longest is exactly 512. `decay_rate`: positive rates.
All inputs are finite; a program needn't handle non-finite values.
Results may differ from a plain program's by a relative error of at most 0.03.
Values may be sent and summed in bfloat16 or wider, within the bound.
A program may use at most 64 MiB of HBM per device.

v0:
```python
import jax
import jax.numpy as jnp
import numpy as np
from jax import lax
from jax.sharding import PartitionSpec as P

HDIM = 64
GROUPS = 8
STATE = 128
CONV = 4
STRETCH = 256
INNER = 8192
HIGH = lax.Precision.HIGHEST


def from_behind(x, axis, by):
    count = lax.axis_size(axis)
    pairs = [(i, i + by) for i in range(count) if 0 <= i + by < count]
    return lax.ppermute(x, axis, pairs)


def carried_in(x, axis, combine, identity):
    count, here = (lax.axis_size(axis), lax.axis_index(axis))
    everything = jax.tree.map(
        lambda part, kind: lax.all_gather(part.astype(kind), axis), x, (jnp.bfloat16, jnp.bfloat16)
    )
    start = jax.tree.map(
        lambda part, zero: jnp.broadcast_to(jnp.asarray(zero, part.dtype), part.shape), x, identity
    )

    def hop(k, before):
        reached = k < here
        new = combine(
            before, jax.tree.map(lambda part, own: part[k].astype(own.dtype), everything, x)
        )
        return jax.tree.map(lambda a, b: jnp.where(reached, a, b), new, before)

    return lax.fori_loop(0, count, hop, start)


def doc_ids(lengths, positions):
    starts = jnp.cumsum(lengths) - lengths
    counted = jnp.sum((starts[None, :] <= positions[:, None]).astype(jnp.int32), axis=1)
    return counted - 1


def causal_conv(values, edge, weights, bias, docs, edge_docs):
    count = values.shape[0]
    extended = jnp.concatenate([edge, values], axis=0).astype(jnp.float32)
    all_docs = jnp.concatenate([edge_docs, docs])
    summed = jnp.zeros(values.shape, jnp.float32) + bias[None, :]
    for offset in range(weights.shape[0]):
        same = (all_docs[offset : offset + count] == docs).astype(jnp.float32)
        summed = (
            summed + weights[offset][None, :] * extended[offset : offset + count] * same[:, None]
        )
    return lax.optimization_barrier(jax.nn.silu(summed).astype(jnp.bfloat16))


def ssd_blocks(xvals, dtv, rate, bmat, cmat, docs, prev_doc, head_group, block):
    count, heads, hdim = xvals.shape
    nstate = bmat.shape[2]
    blocks = count // block
    logs = -dtv * rate[None, :]

    def split(array):
        return array.reshape((blocks, block) + array.shape[1:])

    lower = jnp.tril(jnp.ones((block, block), bool))

    def step(carry, pieces):
        state, last_doc = carry
        xblk, dblk, lblk, bblk, cblk, docblk = pieces
        cum = jnp.cumsum(lblk, axis=0)
        same = (docblk[:, None] == docblk[None, :]) & lower
        diff = cum.T[:, :, None] - cum.T[:, None, :]
        decay = jnp.exp(jnp.where(same[None], diff, -jnp.inf))
        scores = jnp.einsum("ign,jgn->gij", cblk, bblk, precision=HIGH)
        mixing = scores[head_group] * decay * dblk.T[:, None, :]
        inner = jnp.einsum("hij,jhp->ihp", mixing, xblk, precision=HIGH)
        open_in = (docblk == last_doc).astype(jnp.float32)
        carry_in = jnp.exp(cum) * open_in[:, None]
        chead = cblk[:, head_group, :]
        outer = jnp.einsum("ihn,hpn->ihp", chead, state, precision=HIGH) * carry_in[:, :, None]
        end_doc = docblk[-1]
        tail = (
            jnp.exp(cum[-1][None, :] - cum)
            * (docblk == end_doc).astype(jnp.float32)[:, None]
            * dblk
        )
        bhead = bblk[:, head_group, :]
        fresh = jnp.einsum("jh,jhp,jhn->hpn", tail, xblk, bhead, precision=HIGH)
        state = carry_in[-1][:, None, None] * state + fresh
        return ((state, end_doc), inner + outer)

    init = (jnp.zeros((heads, hdim, nstate), jnp.float32), prev_doc)
    (state, end_doc), outs = lax.scan(
        step, init, (split(xvals), split(dtv), split(logs), split(bmat), split(cmat), split(docs))
    )
    return (outs.reshape(count, heads, hdim), state)


def shards(
    tokens,
    w_gate,
    w_xin,
    w_bc,
    w_dt,
    conv_x,
    conv_x_bias,
    conv_bc,
    conv_bc_bias,
    dt_bias,
    decay_rate,
    d_skip,
    norm_gain,
    w_out,
    lengths,
):
    tensor_count = lax.axis_size("tensor")
    seq_index = lax.axis_index("seq")
    tensor_index = lax.axis_index("tensor")
    span_rows = lax.all_gather(tokens, "tensor", axis=0, tiled=True)
    span_len = span_rows.shape[0]
    pieces = (
        lax.all_gather(w_gate, "seq", axis=0, tiled=True),
        lax.all_gather(w_xin, "seq", axis=0, tiled=True),
        lax.all_gather(w_bc, "seq", axis=0, tiled=True),
        lax.all_gather(w_dt, "seq", axis=0, tiled=True),
    )
    gate_acc, xin_acc, bc_acc, dt_acc = tuple(
        (
            jnp.dot(span_rows, weight_piece, preferred_element_type=jnp.float32)
            for weight_piece in pieces
        )
    )
    gate = gate_acc.astype(jnp.bfloat16)
    xin = xin_acc.astype(jnp.bfloat16)
    bcin = bc_acc.astype(jnp.bfloat16)
    dtin = dt_acc.astype(jnp.bfloat16)
    gate, xin, bcin, dtin = lax.optimization_barrier((gate, xin, bcin, dtin))
    positions = seq_index * span_len + jnp.arange(span_len, dtype=jnp.int32)
    docs = doc_ids(lengths, positions)
    edge_docs = doc_ids(lengths, seq_index * span_len + jnp.arange(-(CONV - 1), 0, dtype=jnp.int32))
    prev_span_doc = doc_ids(lengths, positions[:1] - 1)[0]
    edge_x, edge_bc = from_behind(
        (xin[span_len - (CONV - 1) :], bcin[span_len - (CONV - 1) :]), "seq", 1
    )
    x_conv = causal_conv(xin, edge_x, conv_x, conv_x_bias, docs, edge_docs)
    bc_conv = causal_conv(bcin, edge_bc, conv_bc, conv_bc_bias, docs, edge_docs)
    group_span = tensor_count // GROUPS
    my_group = tensor_index // group_span
    every_group = lax.all_gather(bc_conv, "tensor", axis=1, tiled=True)
    arranged = every_group.reshape(span_len, 2 * STATE, GROUPS)
    group_cols = lax.dynamic_slice_in_dim(arranged, my_group, 1, 2).reshape(span_len, 2 * STATE)
    head_dev = w_dt.shape[1]
    head_group = np.zeros(head_dev, dtype=np.int32)
    both = group_cols.astype(jnp.float32)
    bmat = both[:, None, :STATE]
    cmat = both[:, None, STATE:]
    xvals = x_conv.astype(jnp.float32).reshape(span_len, head_dev, HDIM)
    dtv = jax.nn.softplus(dtin.astype(jnp.float32) + dt_bias[None, :])
    block = min(STRETCH, span_len)
    y_local, end_state = ssd_blocks(
        xvals, dtv, decay_rate, bmat, cmat, docs, prev_span_doc, head_group, block
    )
    cum_span = jnp.cumsum(-dtv * decay_rate[None, :], axis=0)
    open_span = (docs == prev_span_doc).astype(jnp.float32)
    span_decay = jnp.exp(cum_span[-1]) * open_span[-1]

    def combine(earlier, later):
        return (earlier[0] * later[0], later[0][:, None, None] * earlier[1] + later[1])

    entering = carried_in(
        (span_decay, end_state),
        "seq",
        combine,
        (jnp.ones_like(span_decay), jnp.zeros_like(end_state)),
    )[1]
    carried = jnp.exp(cum_span) * open_span[:, None]
    y_enter = (
        jnp.einsum("ihn,hpn->ihp", cmat[:, head_group, :], entering, precision=HIGH)
        * carried[:, :, None]
    )
    yvals = (y_local + y_enter + d_skip[None, :, None] * xvals).reshape(span_len, head_dev * HDIM)
    gated = yvals * jax.nn.silu(gate.astype(jnp.float32))
    local_sq = jnp.sum(gated * gated, axis=1)
    group_mark = (jnp.arange(GROUPS) == my_group).astype(jnp.float32)
    every_sum = lax.psum(local_sq[:, None] * group_mark[None, :], "tensor")
    group_mean = jnp.sum(every_sum * group_mark[None, :], axis=1) / (INNER // GROUPS)
    normed = (gated * lax.rsqrt(group_mean + 1e-05)[:, None] * norm_gain[None, :]).astype(
        jnp.bfloat16
    )
    w_full = lax.all_gather(w_out, "seq", axis=1, tiled=True)
    return lax.psum_scatter(
        jnp.dot(normed, w_full, preferred_element_type=jnp.float32).astype(jnp.bfloat16),
        "tensor",
        scatter_dimension=0,
        tiled=True,
    )


def solution(mesh):
    in_specs = (
        P(("seq", "tensor"), None),
        P("seq", "tensor"),
        P("seq", "tensor"),
        P("seq", "tensor"),
        P("seq", "tensor"),
        P(None, "tensor"),
        P("tensor"),
        P(None, "tensor"),
        P("tensor"),
        P("tensor"),
        P("tensor"),
        P("tensor"),
        P("tensor"),
        P("tensor", "seq"),
        P(),
    )
    out_specs = P(("seq", "tensor"), None)
    return jax.shard_map(shards, mesh=mesh, in_specs=in_specs, out_specs=out_specs, check_vma=False)
```

profile of v0, /device:TPU:0, one launch (start us, length us, event | category | flops | bytes accessed | tf_op | source)
XLA Modules:
  0.0 462.2 jit_solution(14876827878078978227)
XLA Ops:
  6.5 0.7 all-gather.10.cloned.1.call-update
  7.3 0.7 all-gather.16.cloned.1.call-update
  8.1 0.7 all-gather.12.cloned.1.call-update
  8.8 0.5 all-gather.14.cloned.1.call-update
  9.4 0.5 slice.124
  9.9 0.2 reduce-window.21
  10.8 0.6 fusion.50
  11.4 0.1 convert_reduce_fusion
  11.5 0.6 slice.128
  12.7 9.9 %all_gather.35 = bf16[4096,16]{0,1:T(8,128)(2,1)S(1)} all-gather(bf16[1024,16]{0,1:T(8,128)(2,1)S(1)} %copy-done.2), channel_id=1, replica_groups=mesh['seq'=4,'tensor'=8] {'seq'}, dimensions={0}, use_global_device_ids=true | all-gather | bytes 163840 | tf_op jit(solution)/shard_map/all_gather | solution.py:129
  22.7 0.2 convert_reduce_fusion.1
  22.8 0.1 pad_add_fusion
  22.9 17.9 %all-gather.10.cloned.1.call-done = bf16[256,4096]{1,0:T(8,128)(2,1)} async-done(((bf16[32,4096]{1,0:T(8,128)(2,1)}), bf16[256,4096]{1,0:T(8,128)(2,1)}) %all-gather.10.cloned.1.call-update) | async-done | bytes 2097168 | tf_op jit(solution)/shard_map/all_gather | solution.py:123
  40.8 2.4 convolution_convert_fusion.4
  43.2 34.3 %all-gather.16.cloned.1.call-done = bf16[4096,256]{1,0:T(8,128)(2,1)} async-done(((bf16[1024,256]{1,0:T(8,128)(2,1)}), bf16[4096,256]{1,0:T(8,128)(2,1)}) %all-gather.16.cloned.1.call-update) | async-done | bytes 2097168 | tf_op jit(solution)/shard_map/all_gather | solution.py:128
  77.5 2.3 convolution_convert_fusion.3
  79.8 87.1 %all-gather.12.cloned.1.call-done = bf16[4096,1024]{1,0:T(8,128)(2,1)} async-done(((bf16[1024,1024]{1,0:T(8,128)(2,1)}), bf16[4096,1024]{1,0:T(8,128)(2,1)}) %all-gather.12.cloned.1.call-update) | async-done | bytes 8388624 | tf_op jit(solution)/shard_map/all_gather | solution.py:126
  167.0 6.6 %convolution_convert_fusion.2 = bf16[256,1024]{1,0:T(8,128)(2,1)} fusion(bf16[256,4096]{1,0:T(8,128)(2,1)S(1)} %copy-done, bf16[4096,1024]{1,0:T(8,128)(2,1)} %all-gather.12.cloned.1.call-done), kind=kOutput, calls=%fused_computation.29 | convolution fusion | flops 2147745792 | bytes 11010048 | tf_op jit(solution)/shard_map/dot_general | solution.py:133
  173.5 82.8 %all-gather.14.cloned.1.call-done = bf16[4096,1024]{1,0:T(8,128)(2,1)} async-done(((bf16[1024,1024]{1,0:T(8,128)(2,1)}), bf16[4096,1024]{1,0:T(8,128)(2,1)}) %all-gather.14.cloned.1.call-update) | async-done | bytes 8388624 | tf_op jit(solution)/shard_map/all_gather | solution.py:127
  256.3 5.8 %convolution_convert_fusion.1 = bf16[256,1024]{1,0:T(8,128)(2,1)S(1)} fusion(bf16[256,4096]{1,0:T(8,128)(2,1)S(1)} %copy-done, bf16[4096,1024]{1,0:T(8,128)(2,1)} %all-gather.14.cloned.1.call-done), kind=kOutput, calls=%fused_computation.28 | convolution fusion | flops 2147745792 | bytes 11010048 | tf_op jit(solution)/shard_map/dot_general | solution.py:133
  262.1 3.4 collective-permute-start.1
  265.5 0.7 compare_convert_fusion.6
  266.2 0.6 collective-permute-done.1
  266.8 0.9 multiply_convert_fusion.3
  267.9 0.1 copy_bitcast_fusion.1
  267.9 0.6 reduce-window.22
  268.5 0.2 slice_reduce_fusion
  268.7 4.2 collective-permute-start
  273.0 0.2 slice_reduce_fusion.1
  273.2 0.1 multiply_multiply_fusion
  273.3 0.2 fusion.48
  273.5 0.8 collective-permute-done
  274.3 0.1 maximum_convert_fusion
  274.4 0.8 multiply_convert_fusion.1
  275.3 0.2 copy.38
  275.5 18.1 %all-gather.18.cloned.1.call-done = bf16[256,2048]{1,0:T(8,128)(2,1)} async-done(((bf16[256,256]{1,0:T(8,128)(2,1)}), bf16[256,2048]{1,0:T(8,128)(2,1)}) %all-gather.18.cloned.1.call-update) | async-done | bytes 1048592 | tf_op jit(solution)/shard_map/all_gather | solution.py:153
  293.6 1.5 copy.39
  295.1 0.3 constant_dynamic-slice_fusion
  295.3 0.1 copy.40
  295.5 1.4 fusion.21
  297.0 0.7 all-gather.20.cloned.1.call-update
  297.7 0.6 slice.126
  298.3 0.1 fusion.47
  298.4 0.8 fusion.49
  299.2 7.2 %all-gather.1 = bf16[4,1,16]{2,1,0:T(2,128)(2,1)S(1)} all-gather(bf16[1,1,16]{2,1,0:T(2,128)(2,1)S(1)} %bitcast.101), channel_id=1, replica_groups=mesh['seq'=4,'tensor'=8] {'seq'}, dimensions={0}, use_global_device_ids=true | all-gather | bytes 160 | tf_op jit(solution)/shard_map/all_gather | solution.py:25
  306.4 0.2 fusion.55
  306.5 3.2 fusion.13
  309.7 1.2 fusion.20
  310.9 11.6 %all-gather.22.cloned.1.call-done = bf16[64,64,128]{2,1,0:T(8,128)(2,1)} async-done(((bf16[16,64,128]{2,1,0:T(8,128)(2,1)}), bf16[64,64,128]{2,1,0:T(8,128)(2,1)}) %all-gather.22.cloned.1.call-update) | async-done | bytes 1048592 | tf_op jit(solution)/shard_map/all_gather | solution.py:25
  322.6 4.5 while.9
  322.6 1.1 fusion.74
  323.7 1.1 fusion.74
  324.9 1.1 fusion.74
  326.0 1.1 fusion.74
  327.1 1.3 fusion.18
  328.4 0.3 copy.43
  328.8 0.7 copy-done.1
  329.4 0.4 multiply_reduce_fusion
  329.8 0.1 broadcast_multiply_fusion
  329.9 16.6 %psum.7 = f32[256,8]{0,1:T(8,128)S(1)} all-reduce(f32[256,8]{0,1:T(8,128)S(1)} %broadcast_multiply_fusion), channel_id=1, replica_groups=mesh['seq'=4,'tensor'=8] {'tensor'}, use_global_device_ids=true, to_apply=%region_9.10 | all-reduce | flops 2048 | bytes 16384 | tf_op jit(solution)/shard_map/psum | solution.py:189
  346.5 0.1 multiply_reduce_fusion.1
  346.6 65.5 %all-gather.20.cloned.1.call-done = bf16[1024,4096]{1,0:T(8,128)(2,1)} async-done(((bf16[1024,1024]{1,0:T(8,128)(2,1)}), bf16[1024,4096]{1,0:T(8,128)(2,1)}) %all-gather.20.cloned.1.call-update) | async-done | bytes 8388624 | tf_op jit(solution)/shard_map/all_gather | solution.py:194
  412.1 7.3 %convolution_convert_fusion = bf16[256,4096]{1,0:T(8,128)(2,1)} fusion(bf16[1024,4096]{1,0:T(8,128)(2,1)} %all-gather.20.cloned.1.call-done, f32[1024]{0:T(1024)S(1)} %copy-done.11, f32[256]{0:T(256)S(1)} %add_rsqrt_fusion, f32[256,1024]{1,0:T(8,128)S(1)} %copy.43, bf16[256,1024]{1,0:T(8,128)(2,1)S(1)} %copy-done.1), kind=kOutput, calls=%fused_computation.3 | convolution fusion | flops 2150891520 | bytes 12063744 | tf_op jit(solution)/shard_map/dot_general | solution.py:196
  419.4 36.0 %reduce-scatter.2.cloned.1.call-done = bf16[32,4096]{1,0:T(8,128)(2,1)} async-done(((bf16[256,4096]{1,0:T(8,128)(2,1)}), bf16[32,4096]{1,0:T(8,128)(2,1)}) %reduce-scatter.2.cloned.1.call-update) | async-done | bytes 262160 | tf_op jit(solution)/shard_map/reduce_scatter | solution.py:195
  (55 shorter events, 0.6 us)
Async XLA Ops:
  6.5 34.3 %all-gather.10.cloned.1.call-start = ((), (), s32[]{:S(2)}) async-start(), calls=%async_computation.1 | async-start | bytes 2359296 | tf_op jit(solution)/shard_map/all_gather | solution.py:123
  7.3 70.2 %all-gather.16.cloned.1.call-start = ((), (), s32[]{:S(2)}) async-start(), calls=%async_computation.4 | async-start | bytes 2621440 | tf_op jit(solution)/shard_map/all_gather | solution.py:128
  8.0 1.9 copy-start.8
  8.0 4.7 %copy-start.2 = (bf16[1024,16]{0,1:T(8,128)(2,1)S(1)}, bf16[1024,16]{0,1:T(8,128)(2,1)}, u32[]{:S(2)}) copy-start(bf16[1024,16]{0,1:T(8,128)(2,1)} %param.26) | copy-start | bytes 98308
  8.0 14.9 %copy-start.4 = (f32[4,256]{1,0:T(4,128)S(1)}, f32[4,256]{1,0:T(4,128)}, u32[]{:S(2)}) copy-start(f32[4,256]{1,0:T(4,128)} %param.29) | copy-start | bytes 12292
  8.0 158.9 %all-gather.12.cloned.1.call-start = ((), (), s32[]{:S(2)}) async-start(), calls=%async_computation.2 | async-start | bytes 10485760 | tf_op jit(solution)/shard_map/all_gather | solution.py:126
  8.8 247.5 %all-gather.14.cloned.1.call-start = ((), (), s32[]{:S(2)}) async-start(), calls=%async_computation.3 | async-start | bytes 10485760 | tf_op jit(solution)/shard_map/all_gather | solution.py:127
  9.3 284.2 %all-gather.18.cloned.1.call-start = ((), (), s32[]{:S(2)}) async-start(), calls=%async_computation.5 | async-start | bytes 1179648 | tf_op jit(solution)/shard_map/all_gather | solution.py:153
  40.8 36.7 %copy-start = (bf16[256,4096]{1,0:T(8,128)(2,1)S(1)}, bf16[256,4096]{1,0:T(8,128)(2,1)}, u32[]{:S(2)}) copy-start(bf16[256,4096]{1,0:T(8,128)(2,1)} %all-gather.10.cloned.1.call-done) | copy-start | bytes 6291460
  173.5 93.3 %copy-start.7 = (f32[256]{0:T(256)S(1)}, f32[256]{0:T(256)}, u32[]{:S(2)}) copy-start(f32[256]{0:T(256)} %param.30) | copy-start | bytes 3076
  173.5 94.3 %copy-start.3 = (f32[4,1024]{1,0:T(4,128)S(1)}, f32[4,1024]{1,0:T(4,128)}, u32[]{:S(2)}) copy-start(f32[4,1024]{1,0:T(4,128)} %param.27) | copy-start | bytes 49156
  173.5 94.3 %copy-start.6 = (f32[16]{0:T(128)S(1)}, f32[16]{0:T(128)}, u32[]{:S(2)}) copy-start(f32[16]{0:T(128)} %param.31) | copy-start | bytes 196
  173.5 94.3 %copy-start.9 = (f32[16]{0:T(128)S(1)}, f32[16]{0:T(128)}, u32[]{:S(2)}) copy-start(f32[16]{0:T(128)} %param.32) | copy-start | bytes 196
  262.1 12.4 %copy-start.5 = (f32[1024]{0:T(1024)S(1)}, f32[1024]{0:T(1024)}, u32[]{:S(2)}) copy-start(f32[1024]{0:T(1024)} %param.28) | copy-start | bytes 12292
  262.1 4.7 %collective-permute-start.1 = (bf16[3,256]{1,0:T(4,128)(2,1)S(1)}, bf16[3,256]{1,0:T(4,128)(2,1)S(1)}, u32[]{:S(2)}, u32[]{:S(2)}) collective-permute-start(bf16[3,256]{1,0:T(4,128)(2,1)S(1)} %slice.112), channel_id=1, source_target_pairs={{0,8},{8,16},{16,24},{1,9},{9,17},{17,25},{2,10},{10,18},{18,26},{... | collective-permute-start | bytes 4616 | tf_op jit(solution)/shard_map/ppermute | solution.py:19
  267.7 54.8 %all-gather.22.cloned.1.call-start = ((), (), s32[]{:S(2)}) async-start(), calls=%async_computation.8 | async-start | bytes 1310720 | tf_op jit(solution)/shard_map/all_gather | solution.py:25
  268.7 5.5 %collective-permute-start = (bf16[3,1024]{1,0:T(4,128)(2,1)S(1)}, bf16[3,1024]{1,0:T(4,128)(2,1)S(1)}, u32[]{:S(2)}, u32[]{:S(2)}) collective-permute-start(bf16[3,1024]{1,0:T(4,128)(2,1)S(1)} %slice.100), channel_id=1, source_target_pairs={{0,8},{8,16},{16,24},{1,9},{9,17},{17,25},{2,10},{10,18},{18,26},{... | collective-permute-start | bytes 18440 | tf_op jit(solution)/shard_map/ppermute | solution.py:19
  296.9 115.1 %all-gather.20.cloned.1.call-start = ((), (), s32[]{:S(2)}) async-start(), calls=%async_computation.6 | async-start | bytes 10485760 | tf_op jit(solution)/shard_map/all_gather | solution.py:194
  297.7 157.7 %reduce-scatter.2.cloned.1.call-start = ((), (), s32[]{:S(2)}) async-start(), calls=%async_computation.7 | async-start | bytes 2359296 | tf_op jit(solution)/shard_map/reduce_scatter | solution.py:195
  322.6 4.5 copy-start.10
  328.4 1.0 copy-start.1
  328.4 83.7 %copy-start.11 = (f32[1024]{0:T(1024)S(1)}, f32[1024]{0:T(1024)}, u32[]{:S(2)}) copy-start(f32[1024]{0:T(1024)} %param.34) | copy-start | bytes 12292
Sparse Core Ops, SparseCore 0:
  9.0 31.7 all-gather.9
  42.6 34.7 all-gather.15
  79.3 87.5 all-gather.11
  168.7 87.5 all-gather.13
  267.9 25.6 all-gather.17
  297.0 25.4 all-gather.21
  324.4 87.5 all-gather.19
  419.5 35.7 reduce-scatter.1
where the time goes:
time: 463 us; the launch traced here: 462 us
  waiting for transfers between devices  358 us (77%)
  blocking collectives  33.7 us (7%)
  matrix products  31.6 us (7%)
  between operations  15.1 us (3%)
  other arithmetic  10.7 us (2%)
  starting transfers between devices  7.82 us (2%)
  local copies, waits for them, and re-layouts  5.23 us (1%)
    all_gather x1, waiting for transfers between devices, shards(): lax.all_gather(w_gate, 'seq', axis=0, tiled=True)  87.1 us
    all_gather x1, waiting for transfers between devices, shards(): lax.all_gather(w_xin, 'seq', axis=0, tiled=True)  82.8 us
    all_gather x1, waiting for transfers between devices, shards(): w_full = lax.all_gather(w_out, 'seq', axis=1, tiled=True)  65.5 us
    reduce_scatter x1, waiting for transfers between devices, shards(): lax.psum_scatter(jnp.dot(normed, w_full, preferred_element_type=jnp.float...  36 us
    all_gather x1, waiting for transfers between devices, shards(): lax.all_gather(w_bc, 'seq', axis=0, tiled=True)  34.3 us
    all_gather x1, waiting for transfers between devices, shards(): every_group = lax.all_gather(bc_conv, 'tensor', axis=1, tiled=True)  18.1 us
    all_gather x1, waiting for transfers between devices, shards(): span_rows = lax.all_gather(tokens, 'tensor', axis=0, tiled=True)  17.9 us
    dot_general x4, matrix products, shards(): jnp.dot(span_rows, weight_piece, preferred_element_type=jnp.float32)  17 us
  transfers between devices with their start and end apart: 10, of which 10 were waited for; matrix products, arithmetic and copies ran while one was open for 6% of the time, Pallas kernels for 0%

commit v1 on v0

--- a/solution.py
+++ b/solution.py
@@ -11,6 +11,17 @@
 STRETCH = 256
 INNER = 8192
 HIGH = lax.Precision.HIGHEST
+
+
+def gather_around(array, axis, dim):
+    ways = lax.axis_size(axis)
+    pieces = [array]
+    for far in range(1, ways):
+        pieces.append(
+            lax.ppermute(pieces[far - 1], axis, [(d, (d - 1) % ways) for d in range(ways)])
+        )
+    line = jnp.concatenate(pieces, axis=dim)
+    return jnp.roll(line, lax.axis_index(axis) * array.shape[dim], axis=dim)
 
 
 def from_behind(x, axis, by):
@@ -125,7 +136,7 @@
     pieces = (
         lax.all_gather(w_gate, "seq", axis=0, tiled=True),
         lax.all_gather(w_xin, "seq", axis=0, tiled=True),
-        lax.all_gather(w_bc, "seq", axis=0, tiled=True),
+        gather_around(w_bc, "seq", 0),
         lax.all_gather(w_dt, "seq", axis=0, tiled=True),
     )
     gate_acc, xin_acc, bc_acc, dt_acc = tuple(

time: 463 us -> 427 us (0.922)
  waiting for transfers between devices: 358 us -> 300 us
  starting transfers between devices: 7.82 us -> 18.6 us
  local copies, waits for them, and re-layouts: 5.23 us -> 11.1 us
  blocking collectives: 33.7 us -> 38.6 us
    all_gather x1 -> x0, waiting for transfers between devices: 34.3 us -> none  [shards(): lax.all_gather(w_bc, 'seq', axis=0, tiled=True)]
    all_gather x1, waiting for transfers between devices: 82.8 us -> 64.2 us  [shards(): lax.all_gather(w_xin, 'seq', axis=0, tiled=True)]
    ppermute x0 -> x3, waiting for transfers between devices: none -> 18.5 us  [gather_around(): lax.ppermute(pieces[far - 1], axis, [(d, (d - 1) % ways) for d in range(w...]
    all_gather x1, waiting for transfers between devices: 17.9 us -> 0.01 us  [shards(): span_rows = lax.all_gather(tokens, 'tensor', axis=0, tiled=True)]
    ppermute x0 -> x3, starting transfers between devices: none -> 10.7 us  [gather_around(): lax.ppermute(pieces[far - 1], axis, [(d, (d - 1) % ways) for d in range(w...]
    unnamed x25 -> x33, local copies, waits for them, and re-layouts: 0.73 us -> 6.04 us
  transfers between devices with their start and end apart: 10 -> 12, of which waited for: 10 -> 10; matrix products, arithmetic and copies ran while one was open for 6% -> 8% of each run, Pallas kernels for 0% -> 0%
where the time goes in v1:
time: 427 us; the launch traced here: 426 us
  waiting for transfers between devices  300 us (70%)
  blocking collectives  38.6 us (9%)
  matrix products  30.6 us (7%)
  starting transfers between devices  18.6 us (4%)
  between operations  15.1 us (4%)
  other arithmetic  12.1 us (3%)
  local copies, waits for them, and re-layouts  11.1 us (3%)
    all_gather x1, waiting for transfers between devices, shards(): lax.all_gather(w_gate, 'seq', axis=0, tiled=True)  83.7 us
    all_gather x1, waiting for transfers between devices, shards(): w_full = lax.all_gather(w_out, 'seq', axis=1, tiled=True)  65.1 us
    all_gather x1, waiting for transfers between devices, shards(): lax.all_gather(w_xin, 'seq', axis=0, tiled=True)  64.2 us
    reduce_scatter x1, waiting for transfers between devices, shards(): lax.psum_scatter(jnp.dot(normed, w_full, preferred_element_type=jnp.float...  36 us
    ppermute x3, waiting for transfers between devices, gather_around(): lax.ppermute(pieces[far - 1], axis, [(d, (d - 1) % ways) for d in range(w...  18.5 us
    psum x1, blocking collectives, shards(): every_sum = lax.psum(local_sq[:, None] * group_mark[None, :], 'tensor')  16.6 us
    all_gather x1, waiting for transfers between devices, shards(): every_group = lax.all_gather(bc_conv, 'tensor', axis=1, tiled=True)  16.2 us
    dot_general x4, matrix products, shards(): jnp.dot(span_rows, weight_piece, preferred_element_type=jnp.float32)  16 us
  transfers between devices with their start and end apart: 12, of which 10 were waited for; matrix products, arithmetic and copies ran while one was open for 8% of the time, Pallas kernels for 0%

profile of v1, /device:TPU:0, one launch (start us, length us, event | category | flops | bytes accessed | tf_op | source)
XLA Modules:
  0.0 426.1 jit_solution(5039374048722832855)
XLA Ops:
  6.6 0.7 all-gather.9.cloned.1.call-update
  7.3 0.7 all-gather.13.cloned.1.call-update
  8.1 0.7 all-gather.11.cloned.1.call-update
  8.8 3.9 collective-permute-start
  12.8 0.5 slice.124
  13.9 0.2 reduce-window.21
  14.1 0.7 fusion.58
  14.9 0.8 constant_dynamic-update-slice_fusion.7
  15.7 8.2 %collective-permute-done = bf16[1024,256]{1,0:T(8,128)(2,1)S(1)} collective-permute-done((bf16[1024,256]{1,0:T(8,128)(2,1)S(1)}, bf16[1024,256]{1,0:T(8,128)(2,1)S(1)}, u32[]{:S(2)}, u32[]{:S(2)}) %collective-permute-start) | collective-permute-done | bytes 524320 | tf_op jit(solution)/shard_map/ppermute | solution.py:21
  23.9 3.4 collective-permute-start.1
  27.3 0.2 convert_reduce_fusion.1
  27.5 10.2 %collective-permute-done.1 = bf16[1024,256]{1,0:T(8,128)(2,1)S(1)} collective-permute-done((bf16[1024,256]{1,0:T(8,128)(2,1)S(1)}, bf16[1024,256]{1,0:T(8,128)(2,1)S(1)}, u32[]{:S(2)}, u32[]{:S(2)}) %collective-permute-start.1) | collective-permute-done | bytes 524320 | tf_op jit(solution)/shard_map/ppermute | solution.py:21
  37.7 3.4 collective-permute-start.2
  41.2 0.6 slice.128
  42.4 13.9 %all_gather.31 = bf16[4096,16]{0,1:T(8,128)(2,1)S(1)} all-gather(bf16[1024,16]{0,1:T(8,128)(2,1)S(1)} %copy-done.2), channel_id=1, replica_groups=mesh['seq'=4,'tensor'=8] {'seq'}, dimensions={0}, use_global_device_ids=true | all-gather | bytes 163840 | tf_op jit(solution)/shard_map/all_gather | solution.py:140
  56.4 0.8 constant_dynamic-update-slice_fusion.6
  57.2 0.8 constant_dynamic-update-slice_fusion.5
  58.1 0.8 constant_dynamic-update-slice_fusion.4
  58.9 0.8 constant_dynamic-update-slice_fusion.3
  59.7 0.9 constant_dynamic-update-slice_fusion.2
  60.6 0.8 constant_dynamic-update-slice_fusion.1
  61.4 0.8 constant_dynamic-update-slice_fusion
  62.2 3.1 fusion.27
  65.4 0.6 convolution_convert_fusion.3
  66.0 64.2 %all-gather.13.cloned.1.call-done = bf16[4096,1024]{1,0:T(8,128)(2,1)} async-done(((bf16[1024,1024]{1,0:T(8,128)(2,1)}), bf16[4096,1024]{1,0:T(8,128)(2,1)}) %all-gather.13.cloned.1.call-update) | async-done | bytes 8388624 | tf_op jit(solution)/shard_map/all_gather | solution.py:138
  130.2 5.7 %convolution_convert_fusion.1 = bf16[256,1024]{1,0:T(8,128)(2,1)S(1)} fusion(bf16[256,4096]{1,0:T(8,128)(2,1)S(1)} %copy-done, bf16[4096,1024]{1,0:T(8,128)(2,1)} %all-gather.13.cloned.1.call-done), kind=kOutput, calls=%fused_computation.30 | convolution fusion | flops 2147745792 | bytes 11010048 | tf_op jit(solution)/shard_map/dot_general | solution.py:144
  136.0 83.7 %all-gather.11.cloned.1.call-done = bf16[4096,1024]{1,0:T(8,128)(2,1)} async-done(((bf16[1024,1024]{1,0:T(8,128)(2,1)}), bf16[4096,1024]{1,0:T(8,128)(2,1)}) %all-gather.11.cloned.1.call-update) | async-done | bytes 8388624 | tf_op jit(solution)/shard_map/all_gather | solution.py:137
  219.7 6.5 %convolution_convert_fusion.2 = bf16[256,1024]{1,0:T(8,128)(2,1)} fusion(bf16[256,4096]{1,0:T(8,128)(2,1)S(1)} %copy-done, bf16[4096,1024]{1,0:T(8,128)(2,1)} %all-gather.11.cloned.1.call-done), kind=kOutput, calls=%fused_computation.31 | convolution fusion | flops 2147745792 | bytes 11010048 | tf_op jit(solution)/shard_map/dot_general | solution.py:144
  226.3 3.4 collective-permute-start.4
  229.7 0.7 compare_convert_fusion.6
  230.4 1.2 collective-permute-done.4
  231.7 1.1 multiply_convert_fusion.3
  233.0 0.6 reduce-window.22
  233.6 0.2 slice_reduce_fusion
  233.9 4.3 %collective-permute-start.3 = (bf16[3,1024]{1,0:T(4,128)(2,1)S(1)}, bf16[3,1024]{1,0:T(4,128)(2,1)S(1)}, u32[]{:S(2)}, u32[]{:S(2)}) collective-permute-start(bf16[3,1024]{1,0:T(4,128)(2,1)S(1)} %slice.100), channel_id=1, source_target_pairs={{0,8},{8,16},{16,24},{1,9},{9,17},{17,25},{2,10},{10,18},{18,26},{... | collective-permute-start | bytes 18440 | tf_op jit(solution)/shard_map/ppermute | solution.py:30
  238.2 0.2 slice_reduce_fusion.1
  238.5 0.2 fusion.56
  238.7 0.8 collective-permute-done.3
  239.6 0.8 multiply_convert_fusion.1
  240.5 0.2 copy.36
  240.7 16.2 %all-gather.15.cloned.1.call-done = bf16[256,2048]{0,1:T(8,128)(2,1)} async-done(((bf16[256,256]{0,1:T(8,128)(2,1)}), bf16[256,2048]{0,1:T(8,128)(2,1)}) %all-gather.15.cloned.1.call-update) | async-done | bytes 1048592 | tf_op jit(solution)/shard_map/all_gather | solution.py:164
  256.9 1.5 constant_dynamic-slice_fusion
  258.4 0.1 copy.42
  258.6 1.4 fusion.23
  260.0 0.5 all-gather.17.cloned.1.call-update
  260.6 0.6 slice.126
  261.3 0.7 fusion.57
  262.0 8.0 %all-gather.1 = bf16[4,1,16]{2,1,0:T(2,128)(2,1)S(1)} all-gather(bf16[1,1,16]{2,1,0:T(2,128)(2,1)S(1)} %bitcast.102), channel_id=1, replica_groups=mesh['seq'=4,'tensor'=8] {'seq'}, dimensions={0}, use_global_device_ids=true | all-gather | bytes 160 | tf_op jit(solution)/shard_map/all_gather | solution.py:36
  270.1 0.2 fusion.64
  270.3 3.2 fusion.15
  273.5 1.2 fusion.22
  274.7 11.7 %all-gather.19.cloned.1.call-done = bf16[64,64,128]{2,1,0:T(8,128)(2,1)} async-done(((bf16[16,64,128]{2,1,0:T(8,128)(2,1)}), bf16[64,64,128]{2,1,0:T(8,128)(2,1)}) %all-gather.19.cloned.1.call-update) | async-done | bytes 1048592 | tf_op jit(solution)/shard_map/all_gather | solution.py:36
  286.4 4.5 %while.9 = (s32[]{:T(128)}, f32[16,64,128]{2,1,0:T(8,128)S(1)}, s32[]{:T(128)}, bf16[4,16]{1,0:T(4,128)(2,1)S(1)}, bf16[4,16,64,128]{3,2,1,0:T(8,128)(2,1)}, /*index=5*/s32[]{:T(128)}, s32[]{:T(128)}) while((s32[]{:T(128)}, f32[16,64,128]{2,1,0:T(8,128)S(1)}, s32[]{:T(128)}, bf16[4,16]{1,0:T(4,128)(2,1)S(1)}, ...), condition=%wide.region_7.8_spmd.clone, body=%wide.region_6.7_spmd.clone.sunk | while | flops 655380 | bytes 1310985 | solution.py:49
  286.4 1.1 fusion.82
  287.5 1.1 fusion.82
  288.6 1.1 fusion.82
  289.8 1.1 fusion.82
  290.9 1.2 fusion.20
  292.1 0.3 copy.40
  292.5 1.4 multiply_reduce_fusion
  294.0 16.6 %psum.7 = f32[256,8]{0,1:T(8,128)S(1)} all-reduce(f32[256,8]{0,1:T(8,128)S(1)} %broadcast_multiply_fusion), channel_id=1, replica_groups=mesh['seq'=4,'tensor'=8] {'tensor'}, use_global_device_ids=true, to_apply=%region_9.10 | all-reduce | flops 2048 | bytes 16384 | tf_op jit(solution)/shard_map/psum | solution.py:200
  310.7 65.1 %all-gather.17.cloned.1.call-done = bf16[1024,4096]{1,0:T(8,128)(2,1)} async-done(((bf16[1024,1024]{1,0:T(8,128)(2,1)}), bf16[1024,4096]{1,0:T(8,128)(2,1)}) %all-gather.17.cloned.1.call-update) | async-done | bytes 8388624 | tf_op jit(solution)/shard_map/all_gather | solution.py:205
  375.7 7.5 %convolution_convert_fusion = bf16[256,4096]{1,0:T(8,128)(2,1)} fusion(bf16[1024,4096]{1,0:T(8,128)(2,1)} %all-gather.17.cloned.1.call-done, f32[1024]{0:T(1024)S(1)} %copy-done.11, f32[256]{0:T(256)S(1)} %add_rsqrt_fusion, f32[256,1024]{1,0:T(8,128)S(1)} %copy.40, bf16[256,1024]{1,0:T(8,128)(2,1)} %convolution_convert_fusion.2), kind=kOutput, calls=%fused_computation.3 | convolution fusion | flops 2150891520 | bytes 12063744 | tf_op jit(solution)/shard_map/dot_general | solution.py:207
  383.3 36.0 %reduce-scatter.2.cloned.1.call-done = bf16[32,4096]{1,0:T(8,128)(2,1)} async-done(((bf16[256,4096]{1,0:T(8,128)(2,1)}), bf16[32,4096]{1,0:T(8,128)(2,1)}) %reduce-scatter.2.cloned.1.call-update) | async-done | bytes 262160 | tf_op jit(solution)/shard_map/reduce_scatter | solution.py:206
  (65 shorter events, 1.5 us)
Async XLA Ops:
  6.5 2.3 copy-start.1
  6.5 7.4 %copy-start.8 = (s32[8]{0:T(128)S(1)}, s32[8]{0:T(128)}, u32[]{:S(2)}) copy-start(s32[8]{0:T(128)} %param.36) | copy-start | bytes 100
  6.5 35.9 %copy-start.2 = (bf16[1024,16]{0,1:T(8,128)(2,1)S(1)}, bf16[1024,16]{0,1:T(8,128)(2,1)}, u32[]{:S(2)}) copy-start(bf16[1024,16]{0,1:T(8,128)(2,1)} %param.26) | copy-start | bytes 98308
  6.5 49.8 %copy-start.4 = (f32[4,256]{1,0:T(4,128)S(1)}, f32[4,256]{1,0:T(4,128)}, u32[]{:S(2)}) copy-start(f32[4,256]{1,0:T(4,128)} %param.29) | copy-start | bytes 12292
  6.5 55.7 %all-gather.9.cloned.1.call-start = ((), (), s32[]{:S(2)}) async-start(), calls=%async_computation.1 | async-start | bytes 2359296 | tf_op jit(solution)/shard_map/all_gather | solution.py:134
  7.3 122.9 %all-gather.13.cloned.1.call-start = ((), (), s32[]{:S(2)}) async-start(), calls=%async_computation.3 | async-start | bytes 10485760 | tf_op jit(solution)/shard_map/all_gather | solution.py:138
  8.0 211.7 %all-gather.11.cloned.1.call-start = ((), (), s32[]{:S(2)}) async-start(), calls=%async_computation.2 | async-start | bytes 10485760 | tf_op jit(solution)/shard_map/all_gather | solution.py:137
  8.8 248.1 %all-gather.15.cloned.1.call-start = ((), (), s32[]{:S(2)}) async-start(), calls=%async_computation.4 | async-start | bytes 1179648 | tf_op jit(solution)/shard_map/all_gather | solution.py:164
  8.8 15.1 %collective-permute-start = (bf16[1024,256]{1,0:T(8,128)(2,1)S(1)}, bf16[1024,256]{1,0:T(8,128)(2,1)S(1)}, u32[]{:S(2)}, u32[]{:S(2)}) collective-permute-start(bf16[1024,256]{1,0:T(8,128)(2,1)S(1)} %copy-done.1), channel_id=1, source_target_pairs={{0,24},{8,0},{16,8},{24,16},{1,25},{9,1},{17,9},{25,17},{2,26},{10... | collective-permute-start | bytes 1572872 | tf_op jit(solution)/shard_map/ppermute | solution.py:21
  23.9 13.8 %collective-permute-start.1 = (bf16[1024,256]{1,0:T(8,128)(2,1)S(1)}, bf16[1024,256]{1,0:T(8,128)(2,1)S(1)}, u32[]{:S(2)}, u32[]{:S(2)}) collective-permute-start(bf16[1024,256]{1,0:T(8,128)(2,1)S(1)} %collective-permute-done), channel_id=1, source_target_pairs={{0,24},{8,0},{16,8},{24,16},{1,25},{9,1},{17,9},{25,17},{2,26},{10... | collective-permute-start | bytes 1572872 | tf_op jit(solution)/shard_map/ppermute | solution.py:21
  37.7 20.3 %collective-permute-start.2 = (bf16[1024,256]{1,0:T(8,128)(2,1)S(1)}, bf16[1024,256]{1,0:T(8,128)(2,1)S(1)}, u32[]{:S(2)}, u32[]{:S(2)}) collective-permute-start(bf16[1024,256]{1,0:T(8,128)(2,1)S(1)} %collective-permute-done.1), channel_id=1, source_target_pairs={{0,24},{8,0},{16,8},{24,16},{1,25},{9,1},{17,9},{25,17},{2,26},{10... | collective-permute-start | bytes 1572872 | tf_op jit(solution)/shard_map/ppermute | solution.py:21
  62.2 3.1 copy-start
  135.9 95.8 %copy-start.7 = (f32[256]{0:T(256)S(1)}, f32[256]{0:T(256)}, u32[]{:S(2)}) copy-start(f32[256]{0:T(256)} %param.30) | copy-start | bytes 3076
  135.9 97.0 %copy-start.3 = (f32[4,1024]{1,0:T(4,128)S(1)}, f32[4,1024]{1,0:T(4,128)}, u32[]{:S(2)}) copy-start(f32[4,1024]{1,0:T(4,128)} %param.27) | copy-start | bytes 49156
  135.9 97.0 %copy-start.6 = (f32[16]{0:T(128)S(1)}, f32[16]{0:T(128)}, u32[]{:S(2)}) copy-start(f32[16]{0:T(128)} %param.31) | copy-start | bytes 196
  135.9 97.0 %copy-start.9 = (f32[16]{0:T(128)S(1)}, f32[16]{0:T(128)}, u32[]{:S(2)}) copy-start(f32[16]{0:T(128)} %param.32) | copy-start | bytes 196
  136.0 103.7 %copy-start.5 = (f32[1024]{0:T(1024)S(1)}, f32[1024]{0:T(1024)}, u32[]{:S(2)}) copy-start(f32[1024]{0:T(1024)} %param.28) | copy-start | bytes 12292
  226.3 5.3 %collective-permute-start.4 = (bf16[3,256]{0,1:T(8,128)(2,1)S(1)}, bf16[3,256]{0,1:T(8,128)(2,1)S(1)}, u32[]{:S(2)}, u32[]{:S(2)}) collective-permute-start(bf16[3,256]{0,1:T(8,128)(2,1)S(1)} %slice.112), channel_id=1, source_target_pairs={{0,8},{8,16},{16,24},{1,9},{9,17},{17,25},{2,10},{10,18},{18,26},{... | collective-permute-start | bytes 4616 | tf_op jit(solution)/shard_map/ppermute | solution.py:30
  232.8 53.5 %all-gather.19.cloned.1.call-start = ((), (), s32[]{:S(2)}) async-start(), calls=%async_computation.7 | async-start | bytes 1310720 | tf_op jit(solution)/shard_map/all_gather | solution.py:36
  233.9 5.6 %collective-permute-start.3 = (bf16[3,1024]{1,0:T(4,128)(2,1)S(1)}, bf16[3,1024]{1,0:T(4,128)(2,1)S(1)}, u32[]{:S(2)}, u32[]{:S(2)}) collective-permute-start(bf16[3,1024]{1,0:T(4,128)(2,1)S(1)} %slice.100), channel_id=1, source_target_pairs={{0,8},{8,16},{16,24},{1,9},{9,17},{17,25},{2,10},{10,18},{18,26},{... | collective-permute-start | bytes 18440 | tf_op jit(solution)/shard_map/ppermute | solution.py:30
  260.0 115.8 %all-gather.17.cloned.1.call-start = ((), (), s32[]{:S(2)}) async-start(), calls=%async_computation.5 | async-start | bytes 10485760 | tf_op jit(solution)/shard_map/all_gather | solution.py:205
  260.5 158.7 %reduce-scatter.2.cloned.1.call-start = ((), (), s32[]{:S(2)}) async-start(), calls=%async_computation.6 | async-start | bytes 2359296 | tf_op jit(solution)/shard_map/reduce_scatter | solution.py:206
  273.4 17.4 %copy-start.10 = (f32[16]{0:T(128)S(1)}, f32[16]{0:T(128)}, u32[]{:S(2)}) copy-start(f32[16]{0:T(128)} %param.33) | copy-start | bytes 196
  290.9 84.8 %copy-start.11 = (f32[1024]{0:T(1024)S(1)}, f32[1024]{0:T(1024)}, u32[]{:S(2)}) copy-start(f32[1024]{0:T(1024)} %param.34) | copy-start | bytes 12292
Sparse Core Ops, SparseCore 0:
  9.0 31.7 all-gather.8
  42.6 87.5 all-gather.12
  132.1 87.5 all-gather.10
  233.0 23.8 all-gather.14
  260.1 26.2 all-gather.18
  288.1 87.5 all-gather.16
  383.4 35.7 reduce-scatter.1
